TPU v7x, 512 devices: a whole 4x8x8 slice. The times are simulated.
512 devices in a mesh: seq: 64 (over z, x, core), head: 8 (over y).
Axes of the slice: x: 4, y: 8, z: 8, core: 2. Of those that a mesh axis runs over, the one named last changes fastest.
Arguments:
- loaded: bfloat16 [8192, 2048], P('seq', 'head'), may hold values from -6 to 6
- out_grad: bfloat16 [8192, 2048], P('seq', 'head'), may hold values from -6 to 6
- w_query: bfloat16 [2048, 2048], P(None, 'head'), may hold values from -0.125 to 0.125
- w_key: bfloat16 [2048, 2048], P(None, 'head'), may hold values from -0.125 to 0.125
- w_value: bfloat16 [2048, 2048], P(None, 'head'), may hold values from -0.125 to 0.125
- w_beta: bfloat16 [2048, 16], P(None, 'head'), may hold values from -0.125 to 0.125
- beta_max: float32 [16], P('head'), may hold values from 0.015625 to 1
- out_gain: float32 [128], replicated, may hold values from 0.1 to 1.9
- clip_lengths: int32 [16], replicated, may hold values from 1 to 2048, 8192 in all
- delay_offsets: int32 [4], replicated, may hold values from 0 to 3, each once
- block_order: int32 [64, 64], P('seq'), may hold values from 0 to 63, each once within a row
Outputs:
- head_out: bfloat16 [8192, 2048], P('seq', 'head')
- input_grad: bfloat16 [8192, 2048], P('seq', 'head')
Inputs may be any that keep to these rules, and one draw needn't show every extreme that they name: `clip_lengths`: the clip lengths sum to 8192; the longest is exactly 2048. `delay_offsets`: each codebook has a different delay. `block_order`: each row is a permutation of 0 to 63.
All inputs are finite; a program needn't handle non-finite values.
Results may differ from a plain program's by a relative error of at most 0.022.
Values may be sent and summed in bfloat16 or wider, within the bound.
A program may use at most 128 MiB of HBM per device.

v0:
```python
import jax
import jax.numpy as jnp
from jax import lax
from jax.sharding import PartitionSpec as P

SPAN = 128
EPSILON = 1e-06
HIGHEST = lax.Precision.HIGHEST


def from_behind(x, axis, by):
    count = lax.axis_size(axis)
    pairs = [(i, i + by) for i in range(count) if 0 <= i + by < count]
    return lax.ppermute(x, axis, pairs)


def prefix(x, axis, join, neutral):
    place = lax.axis_index(axis)
    gathered = jax.tree.map(
        lambda a, kind: lax.all_gather(a.astype(kind), axis), x, (jnp.bfloat16, jnp.bfloat16)
    )
    state = jax.tree.map(lambda a, e: jnp.zeros_like(a) + jnp.asarray(e, a.dtype), x, neutral)

    def one(turn, state):
        return join(
            state,
            jax.tree.map(
                lambda a, own: lax.dynamic_index_in_dim(a, turn, 0, False).astype(own.dtype),
                gathered,
                x,
            ),
        )

    return lax.fori_loop(0, place, one, state)


def prefix_2(x, axis, combine, identity):
    count, here = (lax.axis_size(axis), lax.axis_index(axis))
    everything = jax.tree.map(
        lambda part, kind: lax.all_gather(part.astype(kind), axis),
        x,
        jax.tree.map(lambda a: jnp.bfloat16 if a.dtype == jnp.float32 else a.dtype, x),
    )
    start = jax.tree.map(
        lambda part, zero: jnp.broadcast_to(jnp.asarray(zero, part.dtype), part.shape), x, identity
    )

    def turn(k, before):
        at = count - 1 - k
        reached = at > here
        new = combine(
            before, jax.tree.map(lambda part, own: part[at].astype(own.dtype), everything, x)
        )
        return jax.tree.map(lambda a, b: jnp.where(reached, a, b), new, before)

    return lax.fori_loop(0, count, turn, start)


def clip_start(clip_lengths, positions):
    clip_ends = jnp.cumsum(clip_lengths)
    finished = clip_ends[None, :] <= positions[:, None]
    return jnp.sum(jnp.where(finished, clip_lengths[None, :], 0), axis=1)


def column_delays(delay_offsets, columns, group_width):
    codebook = columns // group_width
    matches = codebook[:, None] == jnp.arange(delay_offsets.shape[0], dtype=jnp.int32)[None, :]
    return jnp.sum(jnp.where(matches, delay_offsets[None, :], 0), axis=1)


def prepare(q_raw, k_raw, logit, rate_cap):
    query_rows = q_raw / jnp.sqrt(jnp.sum(q_raw * q_raw, axis=-1, keepdims=True) + EPSILON)
    key_rows = k_raw / jnp.sqrt(jnp.sum(k_raw * k_raw, axis=-1, keepdims=True) + EPSILON)
    beta_rate = rate_cap * jax.nn.sigmoid(logit[:, 0])
    return (query_rows, key_rows, beta_rate)


def span_terms(key_rows, value_rows, beta_rate, clip_begin, span_first):
    span_len = key_rows.shape[0]
    key_width = key_rows.shape[1]
    same_clip = (clip_begin[:, None] == clip_begin[None, :]).astype(jnp.float32)
    gram = beta_rate[:, None] * jnp.dot(key_rows, key_rows.T, precision=HIGHEST) * same_clip
    system = jnp.eye(span_len, dtype=jnp.float32) + jnp.tril(gram, -1)
    stacked = beta_rate[:, None] * jnp.concatenate([key_rows, value_rows], axis=1)
    solved = jax.scipy.linalg.solve_triangular(system, stacked, lower=True, unit_diagonal=True)
    carried = (clip_begin < span_first).astype(jnp.float32)
    final_mask = (clip_begin == clip_begin[-1]).astype(jnp.float32)
    return (solved[:, :key_width], solved[:, key_width:], carried, final_mask, same_clip)


def span_output(state_in, pieces):
    query_rows, key_rows, value_rows, beta_rate, clip_begin, span_first = pieces
    key_part, value_part, carried, final_mask, same_clip = span_terms(
        key_rows, value_rows, beta_rate, clip_begin, span_first
    )
    refreshed = value_part - carried[:, None] * jnp.dot(key_part, state_in, precision=HIGHEST)
    scores = jnp.tril(jnp.dot(query_rows, key_rows.T, precision=HIGHEST)) * same_clip
    outputs = carried[:, None] * jnp.dot(query_rows, state_in, precision=HIGHEST) + jnp.dot(
        scores, refreshed, precision=HIGHEST
    )
    state_out = carried[-1] * state_in + jnp.dot(
        key_rows.T, final_mask[:, None] * refreshed, precision=HIGHEST
    )
    return (state_out, outputs)


def affine_step(affine, pieces):
    key_rows, value_rows, beta_rate, clip_begin, span_first = pieces
    key_part, value_part, carried, final_mask, same_clip = span_terms(
        key_rows, value_rows, beta_rate, clip_begin, span_first
    )
    widened = jnp.concatenate(
        [jnp.zeros((key_rows.shape[0], key_rows.shape[1]), jnp.float32), value_part], axis=1
    )
    refreshed = widened - carried[:, None] * jnp.dot(key_part, affine, precision=HIGHEST)
    return (
        carried[-1] * affine
        + jnp.dot(key_rows.T, final_mask[:, None] * refreshed, precision=HIGHEST),
        None,
    )


def run_head(q_raw, k_raw, v_raw, logit, rate_cap, out_gain, clip_begin, positions, state_in):
    query_rows, key_rows, beta_rate = prepare(q_raw, k_raw, logit, rate_cap)
    span_count = q_raw.shape[0] // SPAN
    pieces = (
        query_rows.reshape(span_count, SPAN, -1),
        key_rows.reshape(span_count, SPAN, -1),
        v_raw.reshape(span_count, SPAN, -1),
        beta_rate.reshape(span_count, SPAN),
        clip_begin.reshape(span_count, SPAN),
        positions.reshape(span_count, SPAN)[:, 0],
    )
    state_out, outputs = lax.scan(span_output, state_in, pieces)
    raw_out = outputs.reshape(-1, outputs.shape[-1])
    normed = (
        raw_out
        / jnp.sqrt(jnp.mean(raw_out * raw_out, axis=-1, keepdims=True) + EPSILON)
        * out_gain[None, :]
    )
    return (normed, state_out)


def compose(before_map, after_map):
    return (
        jnp.matmul(after_map[0], before_map[0], precision=HIGHEST),
        jnp.matmul(after_map[0], before_map[1], precision=HIGHEST) + after_map[1],
    )


def back_product(gradient, weight):
    return lax.dot_general(
        gradient, weight, (((1,), (1,)), ((), ())), preferred_element_type=jnp.float32
    )


def split_heads(matrix, heads_local):
    return matrix.reshape(matrix.shape[0], heads_local, -1).transpose(1, 0, 2)


def join_heads(stacked):
    return stacked.transpose(1, 0, 2).reshape(stacked.shape[1], -1)


def on_device(
    loaded,
    out_grad,
    w_query,
    w_key,
    w_value,
    w_beta,
    beta_max,
    out_gain,
    clip_lengths,
    delay_offsets,
    block_order,
):
    sources = lax.axis_size("seq")
    frames = loaded.shape[0]
    local_width = loaded.shape[1]
    block_rows = frames // sources
    received = lax.all_to_all(
        loaded.reshape(sources, block_rows, local_width),
        "seq",
        split_axis=0,
        concat_axis=0,
        tiled=True,
    )
    inverse = jnp.argsort(block_order[0])
    arranged = jnp.take(received, inverse, axis=0).reshape(frames, local_width)
    positions = lax.axis_index("seq") * frames + jnp.arange(frames, dtype=jnp.int32)
    clip_begin = clip_start(clip_lengths, positions)
    codebooks = delay_offsets.shape[0]
    delay_reach = codebooks - 1
    full_width = local_width * lax.axis_size("head")
    columns = lax.axis_index("head") * local_width + jnp.arange(local_width, dtype=jnp.int32)
    col_delay = column_delays(delay_offsets, columns, full_width // codebooks)
    earlier = from_behind(arranged[frames - delay_reach :], "seq", 1)
    extended = jnp.concatenate([earlier, arranged], axis=0)
    delayed = jnp.zeros((frames, local_width), jnp.bfloat16)
    for shift_by in range(codebooks):
        shifted = extended[delay_reach - shift_by : delay_reach - shift_by + frames]
        inside = positions - shift_by >= clip_begin
        delayed = jnp.where((col_delay[None, :] == shift_by) & inside[:, None], shifted, delayed)
    heads_local = w_beta.shape[1]
    key_width = w_query.shape[1] // heads_local
    value_width = w_value.shape[1] // heads_local
    empty = (
        jnp.zeros((frames, w_query.shape[1]), jnp.float32),
        jnp.zeros((frames, w_key.shape[1]), jnp.float32),
        jnp.zeros((frames, w_value.shape[1]), jnp.float32),
        jnp.zeros((frames, heads_local), jnp.float32),
    )
    feature_part = lax.all_gather(delayed, "head", axis=1, tiled=True)
    results = []
    for running, weight in zip(empty, (w_query, w_key, w_value, w_beta)):
        results.append(jnp.dot(feature_part, weight, preferred_element_type=jnp.float32))
    q_flat, k_flat, v_flat, logit_flat = tuple(results)
    q_heads = split_heads(q_flat, heads_local)
    k_heads = split_heads(k_flat, heads_local)
    v_heads = split_heads(v_flat, heads_local)
    logit_heads = split_heads(logit_flat, heads_local)
    span_count = frames // SPAN
    start_affine = jnp.concatenate(
        [jnp.eye(key_width, dtype=jnp.float32), jnp.zeros((key_width, value_width), jnp.float32)],
        axis=1,
    )

    def head_affine(q_one, k_one, v_one, logit_one, rate_cap):
        query_rows, key_rows, beta_rate = prepare(q_one, k_one, logit_one, rate_cap)
        map_pieces = (
            key_rows.reshape(span_count, SPAN, -1),
            v_one.reshape(span_count, SPAN, -1),
            beta_rate.reshape(span_count, SPAN),
            clip_begin.reshape(span_count, SPAN),
            positions.reshape(span_count, SPAN)[:, 0],
        )
        affine, _ = lax.scan(affine_step, start_affine, map_pieces)
        return affine

    affine = jax.vmap(head_affine)(q_heads, k_heads, v_heads, logit_heads, beta_max)
    transition = affine[:, :, :key_width]
    offset_map = affine[:, :, key_width:]
    identity = (
        jnp.broadcast_to(
            jnp.eye(key_width, dtype=jnp.float32), (heads_local, key_width, key_width)
        ),
        jnp.zeros((heads_local, key_width, value_width), jnp.float32),
    )
    _, state_in = prefix((transition, offset_map), "seq", compose, identity)

    def forward(query_in, key_in, value_in, logit_in, state_start):

        def one_head(q_one, k_one, v_one, logit_one, rate_cap, state_one):
            return run_head(
                q_one, k_one, v_one, logit_one, rate_cap, out_gain, clip_begin, positions, state_one
            )

        return jax.vmap(one_head)(query_in, key_in, value_in, logit_in, beta_max, state_start)

    (normed, state_out), pullback = jax.vjp(
        forward, q_heads, k_heads, v_heads, logit_heads, state_in
    )
    head_out = join_heads(normed).astype(jnp.bfloat16)
    cotangent = split_heads(out_grad, heads_local).astype(jnp.float32)
    first_pass = pullback((cotangent, jnp.zeros_like(state_out)))
    _, state_grad = prefix_2(
        (jnp.swapaxes(transition, 1, 2), first_pass[4]), "seq", compose, identity
    )
    second_pass = pullback((jnp.zeros_like(normed), state_grad))
    gradients = [
        join_heads(first_pass[index] + second_pass[index]).astype(jnp.bfloat16)
        for index in range(4)
    ]
    partial_sum = back_product(gradients[0], w_query) + back_product(gradients[1], w_key)
    partial_sum = (
        partial_sum + back_product(gradients[2], w_value) + back_product(gradients[3], w_beta)
    )
    summed = lax.psum_scatter(
        partial_sum.astype(jnp.bfloat16), "head", scatter_dimension=1, tiled=True
    )
    following = from_behind(summed[:delay_reach], "seq", -1)
    extended_grad = jnp.concatenate([summed, following], axis=0)
    input_grad = jnp.zeros((frames, local_width), jnp.bfloat16)
    for shift_by in range(codebooks):
        ahead = extended_grad[shift_by : shift_by + frames]
        inside = clip_start(clip_lengths, positions + shift_by) <= positions
        input_grad = jnp.where(
            (col_delay[None, :] == shift_by) & inside[:, None], ahead, input_grad
        )
    return (head_out, input_grad)


def solution(mesh):
    return jax.shard_map(
        on_device,
        mesh=mesh,
        in_specs=(
            P("seq", "head"),
            P("seq", "head"),
            P(None, "head"),
            P(None, "head"),
            P(None, "head"),
            P(None, "head"),
            P("head"),
            P(),
            P(),
            P(),
            P("seq", None),
        ),
        out_specs=(P("seq", "head"), P("seq", "head")),
        check_vma=False,
    )
```

profile of v0, /device:TPU:1, one launch (start us, length us, event | category | flops | bytes accessed | tf_op | source)
XLA Modules:
  0.0 574.0 jit_solution(4794235348666533601)
XLA Ops:
  7.2 1.6 reshape.670
  8.9 14.8 %all-to-all-start = ((bf16[64,2,256]{2,1,0:T(2,128)(2,1)}), bf16[64,2,256]{2,1,0:T(2,128)(2,1)S(1)}, u32[]{:S(2)}, u32[]{:S(2)}) async-start(bf16[64,2,256]{2,1,0:T(2,128)(2,1)} %reshape.670), calls=%async_computation | async-start | bytes 131072 | tf_op jit(solution)/shard_map/all_to_all | solution.py:182
  23.8 2.7 sort.17
  27.4 1.3 select_reduce_fusion.2
  30.8 1.9 fusion.106
  35.1 3.5 collective-permute-start
  39.5 21.1 %all_gather.27 = bf16[128,2048]{1,0:T(8,128)(2,1)S(1)} all-gather(bf16[128,256]{1,0:T(8,128)(2,1)S(1)} %and_select_fusion.7), channel_id=1, replica_groups=mesh['seq'=64,'head'=8] {'head'}, dimensions={1}, use_global_device_ids=true | all-gather | bytes 589824 | tf_op jit(solution)/shard_map/all_gather | solution.py:214
  60.7 1.8 multiply_reduce_fusion.10
  64.9 19.7 %custom-call.10 = f32[2,1,128,128]{2,3,1,0:T(8,128)S(1)} custom-call(f32[2,1,128,128]{3,2,1,0:T(8,128)S(1)} %add_bitcast_fusion), custom_call_target="InvertDiagBlocksLowerTriangular" | custom-call | tf_op jit(solution)/shard_map/vmap()/while/body/eval_jaxpr/jit(_solve_triangular)/triangular_solve/custom-call.1 | solution.py:85
  90.5 1.6 copy.156
  94.4 87.9 %all-gather.9.cloned.1.call-done = bf16[128,128,128]{2,1,0:T(8,128)(2,1)} async-done(((bf16[2,128,128]{2,1,0:T(8,128)(2,1)}), bf16[128,128,128]{2,1,0:T(8,128)(2,1)}) %all-gather.9.cloned.1.call-update) | async-done | bytes 4194320 | tf_op jit(solution)/shard_map/all_gather | solution.py:20
  182.3 85.9 %all-gather.11.cloned.1.call-done = bf16[128,128,128]{2,1,0:T(8,128)(2,1)} async-done(((bf16[2,128,128]{2,1,0:T(8,128)(2,1)}), bf16[128,128,128]{2,1,0:T(8,128)(2,1)}) %all-gather.11.cloned.1.call-update) | async-done | bytes 4194320 | tf_op jit(solution)/shard_map/all_gather | solution.py:20
  268.3 1.1 while.25
  275.7 1.1 fusion.63
  278.9 74.5 %all-gather.13.cloned.1.call-done = bf16[128,128,128]{2,1,0:T(8,128)(2,1)} async-done(((bf16[2,128,128]{2,1,0:T(8,128)(2,1)}), bf16[128,128,128]{2,1,0:T(8,128)(2,1)}) %all-gather.13.cloned.1.call-update) | async-done | bytes 4194320 | tf_op jit(solution)/shard_map/all_gather | solution.py:40
  353.4 86.0 %all-gather.15.cloned.1.call-done = bf16[128,128,128]{2,1,0:T(8,128)(2,1)} async-done(((bf16[2,128,128]{2,1,0:T(8,128)(2,1)}), bf16[128,128,128]{2,1,0:T(8,128)(2,1)}) %all-gather.15.cloned.1.call-update) | async-done | bytes 4194320 | tf_op jit(solution)/shard_map/all_gather | solution.py:40
  439.4 73.4 %while.26 = (s32[]{:T(128)}, f32[2,128,128]{2,1,0:T(8,128)S(1)}, s32[]{:T(128)}, bf16[64,2,128,128]{3,2,1,0:T(8,128)(2,1)}, bf16[64,2,128,128]{3,2,1,0:T(8,128)(...) while((s32[]{:T(128)}, f32[2,128,128]{2,1,0:T(8,128)S(1)}, s32[]{:T(128)}, ...), condition=%wide.region_16.19_spmd.clone, body=%wide.region_15.18_spmd.clone.sunk | while | flops 50495496 | bytes 789149 | solution.py:56
  442.9 1.1 fusion.165
  449.8 1.1 fusion.165
  456.7 1.1 fusion.165
  467.0 1.1 fusion.165
  473.9 1.1 fusion.165
  480.8 1.1 fusion.165
  487.7 1.1 fusion.165
  494.5 1.1 fusion.165
  513.3 1.4 convolution_add_fusion.8
  516.7 1.7 multiply_reduce_fusion.1
  522.9 1.2 fusion.11
  525.2 30.2 %reduce-scatter.2.cloned.1.call-done = bf16[128,256]{1,0:T(8,128)(2,1)} async-done(((bf16[128,2048]{1,0:T(8,128)(2,1)}), bf16[128,256]{1,0:T(8,128)(2,1)}) %reduce-scatter.2.cloned.1.call-update) | async-done | bytes 65552 | tf_op jit(solution)/shard_map/reduce_scatter | solution.py:279
  556.0 7.5 %collective-permute-start.1 = (bf16[3,256]{1,0:T(4,128)(2,1)S(1)}, bf16[3,256]{1,0:T(4,128)(2,1)S(1)}, u32[]{:S(2)}, u32[]{:S(2)}) collective-permute-start(bf16[3,256]{1,0:T(4,128)(2,1)S(1)} %slice.115), channel_id=1, source_target_pairs={{8,0},{16,8},{24,16},{32,24},{40,32},{48,40},{56,48},{64,56},{72,6... | collective-permute-start | bytes 4616 | tf_op jit(solution)/shard_map/ppermute | solution.py:14
  564.4 1.5 collective-permute-done.1
  565.9 1.6 and_select_fusion.3
  (329 shorter events, 96.3 us)
Async XLA Ops:
  7.2 85.9 %copy-start = (bf16[2048,256]{1,0:T(8,128)(2,1)S(1)}, bf16[2048,256]{1,0:T(8,128)(2,1)}, u32[]{:S(2)}) copy-start(bf16[2048,256]{1,0:T(8,128)(2,1)} %param.23) | copy-start | bytes 3145732
  7.2 56.3 %copy-start.27 = (bf16[2048,2]{0,1:T(2,128)(2,1)S(1)}, bf16[2048,2]{0,1:T(2,128)(2,1)}, u32[]{:S(2)}) copy-start(bf16[2048,2]{0,1:T(2,128)(2,1)} %param.26) | copy-start | bytes 24580
  7.2 56.3 %copy-start.44 = (f32[2]{0:T(128)S(1)}, f32[2]{0:T(128)}, u32[]{:S(2)}) copy-start(f32[2]{0:T(128)} %param.27) | copy-start | bytes 28
  7.2 77.4 %copy-start.2 = (bf16[2048,256]{1,0:T(8,128)(2,1)S(1)}, bf16[2048,256]{1,0:T(8,128)(2,1)}, u32[]{:S(2)}) copy-start(bf16[2048,256]{1,0:T(8,128)(2,1)} %param.25) | copy-start | bytes 3145732
  8.9 25.4 %all-to-all-start = ((bf16[64,2,256]{2,1,0:T(2,128)(2,1)}), bf16[64,2,256]{2,1,0:T(2,128)(2,1)S(1)}, u32[]{:S(2)}, u32[]{:S(2)}) async-start(bf16[64,2,256]{2,1,0:T(2,128)(2,1)} %reshape.670), calls=%async_computation | async-start | bytes 131072 | tf_op jit(solution)/shard_map/all_to_all | solution.py:182
  23.7 158.6 %all-gather.9.cloned.1.call-start = ((), (), s32[]{:S(2)}) async-start(), calls=%async_computation.3 | async-start | bytes 4259840 | tf_op jit(solution)/shard_map/all_gather | solution.py:20
  30.7 33.6 %copy-start.31 = (pred[256]{0:T(512)(128)(4,1)}, pred[256]{0:T(512)(128)(4,1)S(1)}, u32[]{:S(2)}) copy-start(pred[256]{0:T(512)(128)(4,1)S(1)} %get-tuple-element.999) | copy-start | bytes 772
  30.7 33.6 %copy-start.33 = (pred[256]{0:T(512)(128)(4,1)}, pred[256]{0:T(512)(128)(4,1)S(1)}, u32[]{:S(2)}) copy-start(pred[256]{0:T(512)(128)(4,1)S(1)} %get-tuple-element.1000) | copy-start | bytes 772
  30.7 33.6 %copy-start.35 = (pred[256]{0:T(512)(128)(4,1)}, pred[256]{0:T(512)(128)(4,1)S(1)}, u32[]{:S(2)}) copy-start(pred[256]{0:T(512)(128)(4,1)S(1)} %get-tuple-element.1001) | copy-start | bytes 772
  30.7 33.6 %copy-start.37 = (pred[256]{0:T(512)(128)(4,1)}, pred[256]{0:T(512)(128)(4,1)S(1)}, u32[]{:S(2)}) copy-start(pred[256]{0:T(512)(128)(4,1)S(1)} %get-tuple-element.1002) | copy-start | bytes 772
  35.1 4.3 collective-permute-start
  39.5 52.6 %copy-start.16 = (bf16[128,256]{1,0:T(8,128)(2,1)S(1)}, bf16[128,256]{1,0:T(8,128)(2,1)}, u32[]{:S(2)}) copy-start(bf16[128,256]{1,0:T(8,128)(2,1)} %param.22) | copy-start | bytes 196612
  63.5 30.9 %copy-start.4 = (f32[2,128,128]{1,2,0:T(8,128)}, f32[2,128,128]{1,2,0:T(8,128)S(1)}, u32[]{:S(2)}) copy-start(f32[2,128,128]{1,2,0:T(8,128)S(1)} %bitcast_divide_fusion.4) | copy-start | bytes 393220
  84.6 8.4 %copy-start.29 = (f32[128]{0:T(128)S(1)}, f32[128]{0:T(128)}, u32[]{:S(2)}) copy-start(f32[128]{0:T(128)} %param.28) | copy-start | bytes 1540
  84.6 8.9 %copy-start.18 = (f32[2,128]{1,0:T(2,128)S(1)}, f32[2,128]{1,0:T(2,128)}, u32[]{:S(2)}) copy-start(f32[2,128]{1,0:T(2,128)} %copy-done.17) | copy-start | bytes 3076
  84.7 8.9 %copy-start.39 = (f32[128]{0:T(128)S(1)}, f32[128]{0:T(128)}, u32[]{:S(2)}) copy-start(f32[128]{0:T(128)} %get-tuple-element.1004) | copy-start | bytes 1540
  88.0 181.5 %copy-start.21 = (f32[128]{0:T(128)S(1)}, f32[128]{0:T(128)}, u32[]{:S(2)}) copy-start(f32[128]{0:T(128)} %copy-done.20) | copy-start | bytes 1540
  89.7 178.6 %all-gather.11.cloned.1.call-start = ((), (), s32[]{:S(2)}) async-start(), calls=%async_computation.4 | async-start | bytes 4259840 | tf_op jit(solution)/shard_map/all_gather | solution.py:20
  90.4 263.0 %all-gather.13.cloned.1.call-start = ((), (), s32[]{:S(2)}) async-start(), calls=%async_computation.5 | async-start | bytes 4259840 | tf_op jit(solution)/shard_map/all_gather | solution.py:40
  92.0 347.4 %all-gather.15.cloned.1.call-start = ((), (), s32[]{:S(2)}) async-start(), calls=%async_computation.6 | async-start | bytes 4259840 | tf_op jit(solution)/shard_map/all_gather | solution.py:40
  94.4 179.9 %copy-start.15 = (f32[2,128,128]{2,1,0:T(8,128)}, f32[2,128,128]{2,1,0:T(8,128)S(1)}, u32[]{:S(2)}) copy-start(f32[2,128,128]{2,1,0:T(8,128)S(1)} %fusion.25) | copy-start | bytes 393220
  268.2 6.6 %copy-start.19 = (f32[2,128]{1,0:T(2,128)S(1)}, f32[2,128]{1,0:T(2,128)}, u32[]{:S(2)}) copy-start(f32[2,128]{1,0:T(2,128)} %copy-done.17) | copy-start | bytes 3076
  272.7 282.6 %reduce-scatter.2.cloned.1.call-start = ((), (), s32[]{:S(2)}) async-start(), calls=%async_computation.2 | async-start | bytes 589824 | tf_op jit(solution)/shard_map/reduce_scatter | solution.py:279
  276.8 237.9 %copy-start.22 = (f32[128]{0:T(128)S(1)}, f32[128]{0:T(128)}, u32[]{:S(2)}) copy-start(f32[128]{0:T(128)} %copy-done.20) | copy-start | bytes 1540
  278.4 238.3 %copy-start.24 = (f32[2,128]{1,0:T(2,128)S(1)}, f32[2,128]{1,0:T(2,128)}, u32[]{:S(2)}) copy-start(f32[2,128]{1,0:T(2,128)} %copy-done.23) | copy-start | bytes 3076
  513.3 8.0 %copy-start.43 = (f32[2,128]{1,0:T(2,128)S(1)}, f32[2,128]{1,0:T(2,128)}, u32[]{:S(2)}) copy-start(f32[2,128]{1,0:T(2,128)} %get-tuple-element.988) | copy-start | bytes 3076
  521.8 44.1 %copy-start.32 = (pred[256]{0:T(512)(128)(4,1)S(1)}, pred[256]{0:T(512)(128)(4,1)}, u32[]{:S(2)}) copy-start(pred[256]{0:T(512)(128)(4,1)} %copy-done.31) | copy-start | bytes 772
  521.8 44.1 %copy-start.34 = (pred[256]{0:T(512)(128)(4,1)S(1)}, pred[256]{0:T(512)(128)(4,1)}, u32[]{:S(2)}) copy-start(pred[256]{0:T(512)(128)(4,1)} %copy-done.33) | copy-start | bytes 772
  521.8 44.0 %copy-start.36 = (pred[256]{0:T(512)(128)(4,1)S(1)}, pred[256]{0:T(512)(128)(4,1)}, u32[]{:S(2)}) copy-start(pred[256]{0:T(512)(128)(4,1)} %copy-done.35) | copy-start | bytes 772
  521.8 44.0 %copy-start.38 = (pred[256]{0:T(512)(128)(4,1)S(1)}, pred[256]{0:T(512)(128)(4,1)}, u32[]{:S(2)}) copy-start(pred[256]{0:T(512)(128)(4,1)} %copy-done.37) | copy-start | bytes 772
  521.8 44.0 %copy-start.41 = (pred[128]{0:T(512)(128)(4,1)S(1)}, pred[128]{0:T(512)(128)(4,1)}, u32[]{:S(2)}) copy-start(pred[128]{0:T(512)(128)(4,1)} %get-tuple-element.1003) | copy-start | bytes 388
  556.0 9.8 %collective-permute-start.1 = (bf16[3,256]{1,0:T(4,128)(2,1)S(1)}, bf16[3,256]{1,0:T(4,128)(2,1)S(1)}, u32[]{:S(2)}, u32[]{:S(2)}) collective-permute-start(bf16[3,256]{1,0:T(4,128)(2,1)S(1)} %slice.115), channel_id=1, source_target_pairs={{8,0},{16,8},{24,16},{32,24},{40,32},{48,40},{56,48},{64,56},{72,6... | collective-permute-start | bytes 4616 | tf_op jit(solution)/shard_map/ppermute | solution.py:14
  (25 other events, 80.9 us)
Sparse Core Ops, SparseCore 0:
  89.8 92.4 all-gather.8
  186.3 81.9 all-gather.10
  271.6 81.7 all-gather.12
  357.2 82.2 all-gather.14
  524.2 31.0 reduce-scatter.1
where the time goes:
time: 581 us; the launch traced here: 574 us
  waiting for transfers between devices  367 us (63%)
  matrix products  98.1 us (17%)
  other arithmetic  30.5 us (5%)
  starting transfers between devices  26.2 us (5%)
  blocking collectives  21.1 us (4%)
  between operations  15.6 us (3%)
  local copies, waits for them, and re-layouts  12.1 us (2%)
    all_gather x2, waiting for transfers between devices, prefix(): lax.all_gather(a.astype(kind), axis)  174 us
    all_gather x2, waiting for transfers between devices, prefix_2(): lax.all_gather(part.astype(kind), axis)  161 us
    dot_general x65, matrix products, compose(): jnp.matmul(after_map[0], before_map[1], precision=HIGHEST) + after_map[1]  71 us
    reduce_scatter x1, waiting for transfers between devices, on_device(): lax.psum_scatter(partial_sum.astype(jnp.bfloat16), 'head', scatter_dimens...  30.2 us
    all_gather x1, blocking collectives, on_device(): feature_part = lax.all_gather(delayed, 'head', axis=1, tiled=True)  21.1 us
    another operation x5, other arithmetic, span_terms(): jax.scipy.linalg.solve_triangular(system, stacked, lower=True, unit_diago...  19.9 us
    all_to_all x1, starting transfers between devices, on_device(): lax.all_to_all(loaded.reshape(sources, block_rows, local_width), 'seq', s...  14.8 us
  transfers between devices with their start and end apart: 8, of which 7 were waited for; matrix products, arithmetic and copies ran while one was open for 4% of the time, Pallas kernels for 0%

commit v1 on v0

--- a/solution.py
+++ b/solution.py
@@ -211,7 +211,16 @@
         jnp.zeros((frames, w_value.shape[1]), jnp.float32),
         jnp.zeros((frames, heads_local), jnp.float32),
     )
-    feature_part = lax.all_gather(delayed, "head", axis=1, tiled=True)
+    ways = lax.axis_size("head")
+    up = [(d, (d + 1) % ways) for d in range(ways)]
+    down = [(d, (d - 1) % ways) for d in range(ways)]
+    earlier_2, later = ([delayed], [delayed])
+    for __2 in range(ways // 2):
+        earlier_2.append(lax.ppermute(earlier_2[-1], "head", up))
+    for __2 in range((ways - 1) // 2):
+        later.append(lax.ppermute(later[-1], "head", down))
+    line = jnp.concatenate([*earlier_2[::-1], *later[1:]], axis=1)
+    feature_part = jnp.roll(line, (lax.axis_index("head") - ways // 2) * delayed.shape[1], axis=1)
     results = []
     for running, weight in zip(empty, (w_query, w_key, w_value, w_beta)):
         results.append(jnp.dot(feature_part, weight, preferred_element_type=jnp.float32))

time: 581 us -> 583 us (level)
  starting transfers between devices: 26.2 us -> 47.9 us
  blocking collectives: 21.1 us -> 0 us
  waiting for transfers between devices: 367 us -> 373 us
    ppermute x0 -> x7, starting transfers between devices: none -> 22.8 us  [the longest x3 13.8 us: on_device(): later.append(lax.ppermute(later[-1], 'head', down))]
    all_gather x1 -> x0, blocking collectives: 21.1 us -> none  [on_device(): feature_part = lax.all_gather(delayed, 'head', axis=1, tiled=True)]
  transfers between devices with their start and end apart: 8 -> 15, of which waited for: 7 -> 10; matrix products, arithmetic and copies ran while one was open for 4% -> 4% of each run, Pallas kernels for 0% -> 0%
where the time goes in v1:
time: 583 us; the launch traced here: 576 us
  waiting for transfers between devices  373 us (64%)
  matrix products  95.7 us (16%)
  starting transfers between devices  47.9 us (8%)
  other arithmetic  30.5 us (5%)
  between operations  15.6 us (3%)
  local copies, waits for them, and re-layouts  10.9 us (2%)
    all_gather x2, waiting for transfers between devices, prefix(): lax.all_gather(a.astype(kind), axis)  173 us
    all_gather x2, waiting for transfers between devices, prefix_2(): lax.all_gather(part.astype(kind), axis)  161 us
    dot_general x65, matrix products, compose(): jnp.matmul(after_map[0], before_map[1], precision=HIGHEST) + after_map[1]  71.1 us
    reduce_scatter x1, waiting for transfers between devices, on_device(): lax.psum_scatter(partial_sum.astype(jnp.bfloat16), 'head', scatter_dimens...  30.1 us
    another operation x5, other arithmetic, span_terms(): jax.scipy.linalg.solve_triangular(system, stacked, lower=True, unit_diago...  19.9 us
    all_to_all x1, starting transfers between devices, on_device(): lax.all_to_all(loaded.reshape(sources, block_rows, local_width), 'seq', s...  14.8 us
    ppermute x3, starting transfers between devices, on_device(): later.append(lax.ppermute(later[-1], 'head', down))  13.8 us
  transfers between devices with their start and end apart: 15, of which 10 were waited for; matrix products, arithmetic and copies ran while one was open for 4% of the time, Pallas kernels for 0%

profile of v1, /device:TPU:1, one launch (start us, length us, event | category | flops | bytes accessed | tf_op | source)
XLA Modules:
  0.0 576.3 jit_solution(4453279865362234732)
XLA Ops:
  7.2 1.6 reshape.670
  8.8 14.8 %all-to-all-start = ((bf16[64,2,256]{2,1,0:T(2,128)(2,1)}), bf16[64,2,256]{2,1,0:T(2,128)(2,1)S(1)}, u32[]{:S(2)}, u32[]{:S(2)}) async-start(bf16[64,2,256]{2,1,0:T(2,128)(2,1)} %reshape.670), calls=%async_computation | async-start | bytes 131072 | tf_op jit(solution)/shard_map/all_to_all | solution.py:182
  23.8 2.7 sort.17
  28.1 1.3 select_reduce_fusion.2
  30.6 1.8 fusion.117
  32.6 1.1 all-to-all-done
  34.6 2.4 collective-permute-start
  37.9 3.2 collective-permute-start.1
  41.2 4.2 collective-permute-done.1
  45.4 1.9 collective-permute-start.2
  48.0 4.7 collective-permute-start.5
  52.7 1.9 collective-permute-start.3
  55.3 4.6 collective-permute-start.6
  59.9 1.9 collective-permute-start.4
  61.9 4.6 collective-permute-start.7
  66.6 1.2 collective-permute-done.7
  67.9 1.8 multiply_reduce_fusion.10
  71.6 19.7 %custom-call.10 = f32[2,1,128,128]{2,3,1,0:T(8,128)S(1)} custom-call(f32[2,1,128,128]{3,2,1,0:T(8,128)S(1)} %add_bitcast_fusion), custom_call_target="InvertDiagBlocksLowerTriangular" | custom-call | tf_op jit(solution)/shard_map/vmap()/while/body/eval_jaxpr/jit(_solve_triangular)/triangular_solve/custom-call.1 | solution.py:85
  94.0 1.6 copy.156
  98.0 87.0 %all-gather.11.cloned.1.call-done = bf16[128,128,128]{2,1,0:T(8,128)(2,1)} async-done(((bf16[2,128,128]{2,1,0:T(8,128)(2,1)}), bf16[128,128,128]{2,1,0:T(8,128)(2,1)}) %all-gather.11.cloned.1.call-update) | async-done | bytes 4194320 | tf_op jit(solution)/shard_map/all_gather | solution.py:20
  185.0 85.9 %all-gather.9.cloned.1.call-done = bf16[128,128,128]{2,1,0:T(8,128)(2,1)} async-done(((bf16[2,128,128]{2,1,0:T(8,128)(2,1)}), bf16[128,128,128]{2,1,0:T(8,128)(2,1)}) %all-gather.9.cloned.1.call-update) | async-done | bytes 4194320 | tf_op jit(solution)/shard_map/all_gather | solution.py:20
  270.9 1.1 while.25
  281.4 74.8 %all-gather.13.cloned.1.call-done = bf16[128,128,128]{2,1,0:T(8,128)(2,1)} async-done(((bf16[2,128,128]{2,1,0:T(8,128)(2,1)}), bf16[128,128,128]{2,1,0:T(8,128)(2,1)}) %all-gather.13.cloned.1.call-update) | async-done | bytes 4194320 | tf_op jit(solution)/shard_map/all_gather | solution.py:40
  356.3 85.7 %all-gather.15.cloned.1.call-done = bf16[128,128,128]{2,1,0:T(8,128)(2,1)} async-done(((bf16[2,128,128]{2,1,0:T(8,128)(2,1)}), bf16[128,128,128]{2,1,0:T(8,128)(2,1)}) %all-gather.15.cloned.1.call-update) | async-done | bytes 4194320 | tf_op jit(solution)/shard_map/all_gather | solution.py:40
  442.0 73.4 %while.26 = (s32[]{:T(128)}, f32[2,128,128]{2,1,0:T(8,128)S(1)}, s32[]{:T(128)}, bf16[64,2,128,128]{3,2,1,0:T(8,128)(2,1)}, bf16[64,2,128,128]{3,2,1,0:T(8,128)(...) while((s32[]{:T(128)}, f32[2,128,128]{2,1,0:T(8,128)S(1)}, s32[]{:T(128)}, ...), condition=%wide.region_16.19_spmd.clone, body=%wide.region_15.18_spmd.clone.sunk | while | flops 50495496 | bytes 789157 | solution.py:56
  516.4 1.4 convolution_add_fusion.8
  519.6 1.7 multiply_reduce_fusion.1
  525.3 1.2 fusion.11
  527.6 30.1 %reduce-scatter.2.cloned.1.call-done = bf16[128,256]{1,0:T(8,128)(2,1)} async-done(((bf16[128,2048]{1,0:T(8,128)(2,1)}), bf16[128,256]{1,0:T(8,128)(2,1)}) %reduce-scatter.2.cloned.1.call-update) | async-done | bytes 65552 | tf_op jit(solution)/shard_map/reduce_scatter | solution.py:288
  558.3 7.5 %collective-permute-start.8 = (bf16[3,256]{1,0:T(4,128)(2,1)S(1)}, bf16[3,256]{1,0:T(4,128)(2,1)S(1)}, u32[]{:S(2)}, u32[]{:S(2)}) collective-permute-start(bf16[3,256]{1,0:T(4,128)(2,1)S(1)} %slice.115), channel_id=1, source_target_pairs={{8,0},{16,8},{24,16},{32,24},{40,32},{48,40},{56,48},{64,56},{72,6... | collective-permute-start | bytes 4616 | tf_op jit(solution)/shard_map/ppermute | solution.py:14
  566.7 1.5 collective-permute-done.8
  568.2 1.6 and_select_fusion.3
  (316 shorter events, 102.6 us)
Async XLA Ops:
  7.2 89.4 %copy-start = (bf16[2048,256]{1,0:T(8,128)(2,1)S(1)}, bf16[2048,256]{1,0:T(8,128)(2,1)}, u32[]{:S(2)}) copy-start(bf16[2048,256]{1,0:T(8,128)(2,1)} %param.23) | copy-start | bytes 3145732
  7.2 64.0 %copy-start.19 = (f32[2]{0:T(128)S(1)}, f32[2]{0:T(128)}, u32[]{:S(2)}) copy-start(f32[2]{0:T(128)} %param.27) | copy-start | bytes 28
  7.2 64.0 %copy-start.17 = (bf16[2048,2]{0,1:T(2,128)(2,1)S(1)}, bf16[2048,2]{0,1:T(2,128)(2,1)}, u32[]{:S(2)}) copy-start(bf16[2048,2]{0,1:T(2,128)(2,1)} %param.26) | copy-start | bytes 24580
  8.8 24.9 %all-to-all-start = ((bf16[64,2,256]{2,1,0:T(2,128)(2,1)}), bf16[64,2,256]{2,1,0:T(2,128)(2,1)S(1)}, u32[]{:S(2)}, u32[]{:S(2)}) async-start(bf16[64,2,256]{2,1,0:T(2,128)(2,1)} %reshape.670), calls=%async_computation | async-start | bytes 131072 | tf_op jit(solution)/shard_map/all_to_all | solution.py:182
  23.6 161.3 %all-gather.11.cloned.1.call-start = ((), (), s32[]{:S(2)}) async-start(), calls=%async_computation.4 | async-start | bytes 4259840 | tf_op jit(solution)/shard_map/all_gather | solution.py:20
  34.6 3.2 collective-permute-start
  37.9 7.5 %collective-permute-start.1 = (bf16[128,256]{1,0:T(8,128)(2,1)S(1)}, bf16[128,256]{1,0:T(8,128)(2,1)S(1)}, u32[]{:S(2)}, u32[]{:S(2)}) collective-permute-start(bf16[128,256]{1,0:T(8,128)(2,1)S(1)} %and_select_fusion.7), channel_id=1, source_target_pairs={{0,1},{1,2},{2,3},{3,4},{4,5},{5,6},{6,7},{7,0},{8,9},{9,10},{10,1... | collective-permute-start | bytes 196616 | tf_op jit(solution)/shard_map/ppermute | solution.py:219
  45.4 7.3 %collective-permute-start.2 = (bf16[128,256]{1,0:T(8,128)(2,1)S(1)}, bf16[128,256]{1,0:T(8,128)(2,1)S(1)}, u32[]{:S(2)}, u32[]{:S(2)}) collective-permute-start(bf16[128,256]{1,0:T(8,128)(2,1)S(1)} %collective-permute-done.1), channel_id=1, source_target_pairs={{0,1},{1,2},{2,3},{3,4},{4,5},{5,6},{6,7},{7,0},{8,9},{9,10},{10,1... | collective-permute-start | bytes 196616 | tf_op jit(solution)/shard_map/ppermute | solution.py:219
  48.0 22.6 %copy-start.1 = (bf16[2048,256]{1,0:T(8,128)(2,1)S(1)}, bf16[2048,256]{1,0:T(8,128)(2,1)}, u32[]{:S(2)}) copy-start(bf16[2048,256]{1,0:T(8,128)(2,1)} %param.25) | copy-start | bytes 3145732
  48.0 7.3 %collective-permute-start.5 = (bf16[128,256]{1,0:T(8,128)(2,1)S(1)}, bf16[128,256]{1,0:T(8,128)(2,1)S(1)}, u32[]{:S(2)}, u32[]{:S(2)}) collective-permute-start(bf16[128,256]{1,0:T(8,128)(2,1)S(1)} %and_select_fusion.7), channel_id=1, source_target_pairs={{0,7},{1,0},{2,1},{3,2},{4,3},{5,4},{6,5},{7,6},{8,15},{9,8},{10,9... | collective-permute-start | bytes 196616 | tf_op jit(solution)/shard_map/ppermute | solution.py:221
  52.7 7.2 %collective-permute-start.3 = (bf16[128,256]{1,0:T(8,128)(2,1)S(1)}, bf16[128,256]{1,0:T(8,128)(2,1)S(1)}, u32[]{:S(2)}, u32[]{:S(2)}) collective-permute-start(bf16[128,256]{1,0:T(8,128)(2,1)S(1)} %collective-permute-done.2), channel_id=1, source_target_pairs={{0,1},{1,2},{2,3},{3,4},{4,5},{5,6},{6,7},{7,0},{8,9},{9,10},{10,1... | collective-permute-start | bytes 196616 | tf_op jit(solution)/shard_map/ppermute | solution.py:219
  55.3 6.5 %collective-permute-start.6 = (bf16[128,256]{1,0:T(8,128)(2,1)S(1)}, bf16[128,256]{1,0:T(8,128)(2,1)S(1)}, u32[]{:S(2)}, u32[]{:S(2)}) collective-permute-start(bf16[128,256]{1,0:T(8,128)(2,1)S(1)} %collective-permute-done.5), channel_id=1, source_target_pairs={{0,7},{1,0},{2,1},{3,2},{4,3},{5,4},{6,5},{7,6},{8,15},{9,8},{10,9... | collective-permute-start | bytes 196616 | tf_op jit(solution)/shard_map/ppermute | solution.py:221
  59.9 6.5 %collective-permute-start.4 = (bf16[128,256]{1,0:T(8,128)(2,1)S(1)}, bf16[128,256]{1,0:T(8,128)(2,1)S(1)}, u32[]{:S(2)}, u32[]{:S(2)}) collective-permute-start(bf16[128,256]{1,0:T(8,128)(2,1)S(1)} %collective-permute-done.3), channel_id=1, source_target_pairs={{0,1},{1,2},{2,3},{3,4},{4,5},{5,6},{6,7},{7,0},{8,9},{9,10},{10,1... | collective-permute-start | bytes 196616 | tf_op jit(solution)/shard_map/ppermute | solution.py:219
  61.9 5.9 %collective-permute-start.7 = (bf16[128,256]{1,0:T(8,128)(2,1)S(1)}, bf16[128,256]{1,0:T(8,128)(2,1)S(1)}, u32[]{:S(2)}, u32[]{:S(2)}) collective-permute-start(bf16[128,256]{1,0:T(8,128)(2,1)S(1)} %collective-permute-done.6), channel_id=1, source_target_pairs={{0,7},{1,0},{2,1},{3,2},{4,3},{5,4},{6,5},{7,6},{8,15},{9,8},{10,9... | collective-permute-start | bytes 196616 | tf_op jit(solution)/shard_map/ppermute | solution.py:221
  67.8 28.4 %copy-start.16 = (bf16[128,256]{1,0:T(8,128)(2,1)S(1)}, bf16[128,256]{1,0:T(8,128)(2,1)}, u32[]{:S(2)}) copy-start(bf16[128,256]{1,0:T(8,128)(2,1)} %param.22) | copy-start | bytes 196612
  67.9 28.7 %copy-start.18 = (f32[128]{0:T(128)S(1)}, f32[128]{0:T(128)}, u32[]{:S(2)}) copy-start(f32[128]{0:T(128)} %param.28) | copy-start | bytes 1540
  70.7 27.3 %copy-start.5 = (f32[2,128,128]{1,2,0:T(8,128)}, f32[2,128,128]{1,2,0:T(8,128)S(1)}, u32[]{:S(2)}) copy-start(f32[2,128,128]{1,2,0:T(8,128)S(1)} %bitcast_divide_fusion.4) | copy-start | bytes 393220
  71.2 25.3 %copy-start.4 = (f32[128,256]{0,1:T(8,128)}, f32[128,256]{0,1:T(8,128)S(1)}, u32[]{:S(2)}) copy-start(f32[128,256]{0,1:T(8,128)S(1)} %fusion.30) | copy-start | bytes 393220
  93.2 177.7 %all-gather.9.cloned.1.call-start = ((), (), s32[]{:S(2)}) async-start(), calls=%async_computation.3 | async-start | bytes 4259840 | tf_op jit(solution)/shard_map/all_gather | solution.py:20
  94.0 262.3 %all-gather.13.cloned.1.call-start = ((), (), s32[]{:S(2)}) async-start(), calls=%async_computation.5 | async-start | bytes 4259840 | tf_op jit(solution)/shard_map/all_gather | solution.py:40
  95.6 346.4 %all-gather.15.cloned.1.call-start = ((), (), s32[]{:S(2)}) async-start(), calls=%async_computation.6 | async-start | bytes 4259840 | tf_op jit(solution)/shard_map/all_gather | solution.py:40
  96.6 180.4 %copy-start.24 = (f32[128]{0:T(128)}, f32[128]{0:T(128)S(1)}, u32[]{:S(2)}) copy-start(f32[128]{0:T(128)S(1)} %broadcast_multiply_fusion.3) | copy-start | bytes 1540
  98.0 178.1 %copy-start.15 = (f32[2,128,128]{2,1,0:T(8,128)}, f32[2,128,128]{2,1,0:T(8,128)S(1)}, u32[]{:S(2)}) copy-start(f32[2,128,128]{2,1,0:T(8,128)S(1)} %fusion.25) | copy-start | bytes 393220
  275.3 282.4 %reduce-scatter.2.cloned.1.call-start = ((), (), s32[]{:S(2)}) async-start(), calls=%async_computation.2 | async-start | bytes 589824 | tf_op jit(solution)/shard_map/reduce_scatter | solution.py:288
  515.4 5.9 %copy-start.8 = (f32[2,128,128]{2,1,0:T(8,128)S(1)}, f32[2,128,128]{2,1,0:T(8,128)}, u32[]{:S(2)}) copy-start(f32[2,128,128]{2,1,0:T(8,128)} %copy-done.7) | copy-start | bytes 393220
  515.5 6.2 %copy-start.11 = (f32[2,128,128]{2,1,0:T(8,128)S(1)}, f32[2,128,128]{2,1,0:T(8,128)}, u32[]{:S(2)}) copy-start(f32[2,128,128]{2,1,0:T(8,128)} %copy-done.10) | copy-start | bytes 393220
  515.5 6.5 %copy-start.12 = (f32[2,128,128]{1,2,0:T(8,128)S(1)}, f32[2,128,128]{1,2,0:T(8,128)}, u32[]{:S(2)}) copy-start(f32[2,128,128]{1,2,0:T(8,128)} %fusion.39) | copy-start | bytes 393220
  515.5 6.5 %copy-start.14 = (f32[2,128,128]{2,1,0:T(8,128)S(1)}, f32[2,128,128]{2,1,0:T(8,128)}, u32[]{:S(2)}) copy-start(f32[2,128,128]{2,1,0:T(8,128)} %copy-done.13) | copy-start | bytes 393220
  516.4 7.5 %copy-start.22 = (f32[2,128]{1,0:T(2,128)S(1)}, f32[2,128]{1,0:T(2,128)}, u32[]{:S(2)}) copy-start(f32[2,128]{1,0:T(2,128)} %get-tuple-element.988) | copy-start | bytes 3076
  518.2 6.1 %copy-start.3 = (bf16[2048,256]{1,0:T(8,128)(2,1)S(1)}, bf16[2048,256]{1,0:T(8,128)(2,1)}, u32[]{:S(2)}) copy-start(bf16[2048,256]{1,0:T(8,128)(2,1)} %param.24) | copy-start | bytes 3145732
  524.3 43.9 %copy-start.21 = (pred[128]{0:T(512)(128)(4,1)S(1)}, pred[128]{0:T(512)(128)(4,1)}, u32[]{:S(2)}) copy-start(pred[128]{0:T(512)(128)(4,1)} %get-tuple-element.1003) | copy-start | bytes 388
  558.3 9.8 %collective-permute-start.8 = (bf16[3,256]{1,0:T(4,128)(2,1)S(1)}, bf16[3,256]{1,0:T(4,128)(2,1)S(1)}, u32[]{:S(2)}, u32[]{:S(2)}) collective-permute-start(bf16[3,256]{1,0:T(4,128)(2,1)S(1)} %slice.115), channel_id=1, source_target_pairs={{8,0},{16,8},{24,16},{32,24},{40,32},{48,40},{56,48},{64,56},{72,6... | collective-permute-start | bytes 4616 | tf_op jit(solution)/shard_map/ppermute | solution.py:14
  (11 other events, 30.0 us)
Sparse Core Ops, SparseCore 0:
  93.3 91.5 all-gather.10
  188.9 81.9 all-gather.8
  274.2 82.0 all-gather.12
  360.1 81.8 all-gather.14
  526.7 30.9 reduce-scatter.1
